TPU v7x, 128 devices: a whole 4x4x4 slice. The times are simulated.
128 devices in a mesh: grp: 8 (over y, z_hi), lm: 16 (over x, z_lo, core).
Axes of the slice: x: 4, y: 4, z: 4 (z_hi: 2, z_lo: 2; z = z_hi * 2 + z_lo), core: 2. Of those that a mesh axis runs over, the one named last changes fastest.
Arguments:
- embeddings: bfloat16 [32768, 512], P(('grp', 'lm')), may hold values from -14 to 14
- landmarks: bfloat16 [32768, 512], P('lm'), may hold values from -14 to 14
- start_vectors: float32 [32768, 128], P(('grp', 'lm')), may hold values from -10 to 10
- row_weight: float32 [32768], P(('grp', 'lm')), may hold values from 0.1 to 9
- spread: float32 [1], replicated, may hold values from 11.313708 to 33.941124
Outputs:
- subspace: float32 [32768, 128], P(('grp', 'lm'))
All inputs are finite; a program needn't handle non-finite values.
Results may differ from a plain program's by a relative error of at most 0.019.
Values may be sent and summed in bfloat16 or wider, within the bound.
No kernel may reach another device: no remote copies, remote signals or barrier semaphores. Data moves between devices by JAX's collectives and lax.ppermute only.
A program may use at most 128 MiB of HBM per device.

v0:
```python
import jax
import jax.numpy as jnp
from jax import lax
from jax.sharding import PartitionSpec as P

ITERS = 2


def unit_rows(values):
    values = values.astype(jnp.float32)
    scale = lax.rsqrt(jnp.sum(values * values, axis=1, keepdims=True) + 1e-06)
    return (values * scale).astype(jnp.bfloat16)


def kernel_values(rows_unit, marks_unit, gamma):
    cosine = jnp.einsum("rd,ld->rl", rows_unit, marks_unit, preferred_element_type=jnp.float32)
    return jnp.exp(gamma * cosine)


def local(embeddings, landmarks, start_vectors, row_weight, spread):
    own_rows = embeddings.shape[0]
    marks = landmarks.shape[0]
    groups = lax.axis_size("grp")
    members = lax.axis_size("lm")
    total_rows = own_rows * groups * members
    group_rows = own_rows * members
    gamma = spread[0]
    rows_unit = unit_rows(embeddings)
    marks_unit = unit_rows(landmarks)
    sums = jnp.zeros((marks,), jnp.float32)
    weights = jnp.zeros((group_rows,), jnp.float32)
    part_rows = lax.all_gather(rows_unit, "lm", axis=0, tiled=True)
    part_weight = lax.all_gather(row_weight.astype(jnp.bfloat16), "lm", axis=0, tiled=True).astype(
        jnp.float32
    )
    values = kernel_values(part_rows, marks_unit, gamma)
    build_tile = values.astype(jnp.bfloat16)
    weights = lax.dynamic_update_slice_in_dim(weights, part_weight, jnp.int32(0), 0)
    sums = sums + jnp.sum(part_weight[:, None] * values, axis=0)
    mean_sum, weight_sum = lax.psum((sums, jnp.sum(weights)), "grp")
    means = mean_sum / weight_sum
    vectors = start_vectors
    weighted_full = row_weight[:, None] * vectors
    totals = lax.psum(jnp.sum(weighted_full, axis=0), ("grp", "lm"))
    group_weighted = lax.all_gather(weighted_full.astype(jnp.bfloat16), "lm", axis=0, tiled=True)
    for step in range(ITERS):
        side = (
            lax.psum(
                jnp.einsum(
                    "rl,rv->lv", build_tile, group_weighted, preferred_element_type=jnp.float32
                ),
                "grp",
            )
            - means[:, None] * totals[None, :]
        )
        side_b = side.astype(jnp.bfloat16)
        shift = jnp.dot(means, side_b.astype(jnp.float32), precision=lax.Precision.HIGHEST)
        image = lax.psum_scatter(
            weights[:, None]
            * (jnp.dot(build_tile, side_b, preferred_element_type=jnp.float32) - shift[None, :]),
            "lm",
            scatter_dimension=0,
            tiled=True,
        )
        square, column = lax.psum(
            (jnp.sum(image * image, axis=0), jnp.sum(row_weight[:, None] * image, axis=0)),
            ("grp", "lm"),
        )
        scale = jnp.sqrt(square / total_rows + 1e-06)
        vectors = image / scale[None, :]
        totals = column / scale
        if step + 1 < ITERS:
            group_weighted = lax.all_gather(
                (row_weight[:, None] * vectors).astype(jnp.bfloat16), "lm", axis=0, tiled=True
            )
    return vectors


def solution(mesh):
    in_specs = (
        P(("grp", "lm"), None),
        P("lm", None),
        P(("grp", "lm"), None),
        P(("grp", "lm")),
        P(),
    )
    out_specs = P(("grp", "lm"), None)
    return jax.shard_map(local, mesh=mesh, in_specs=in_specs, out_specs=out_specs, check_vma=False)
```

profile of v0, /device:TPU:1, one launch (start us, length us, event | category | flops | bytes accessed | tf_op | source)
XLA Modules:
  0.0 612.0 jit_solution(1574066524591326856)
XLA Ops:
  6.5 0.0 all-gather.5.cloned.1.call-start
  6.5 1.1 fusion.8
  7.6 1.8 fusion.9
  9.4 0.0 all-gather.5.cloned.1.call-update
  9.4 0.0 all-gather.7.cloned.1.call-start
  9.5 1.6 multiply_reduce_fusion.4
  11.1 0.0 all-gather.7.cloned.1.call-update
  11.1 0.0 all-reduce.5.cloned.1.call-start
  11.2 2.1 fusion.3
  13.3 0.7 convert_element_type.35
  14.0 21.3 %all-gather = bf16[16,1,256]{2,1,0:T(2,128)(2,1)S(1)} all-gather(bf16[1,1,256]{2,1,0:T(2,128)(2,1)S(1)} %reshape.21), channel_id=1, replica_groups=mesh['grp'=8,'lm'=16] {'lm'}, dimensions={0}, use_global_device_ids=true | all-gather | bytes 8704 | tf_op jit(solution)/shard_map/all_gather | solution.py:33
  36.0 14.6 %all-gather.5.cloned.1.call-done = bf16[4096,512]{1,0:T(8,128)(2,1)} async-done(((bf16[256,512]{1,0:T(8,128)(2,1)}), bf16[4096,512]{1,0:T(8,128)(2,1)}) %all-gather.5.cloned.1.call-update) | async-done | bytes 4194320 | tf_op jit(solution)/shard_map/all_gather | solution.py:32
  50.6 16.2 %multiply_reduce_fusion = (f32[2048]{0:T(1024)S(1)}, bf16[4096,2048]{1,0:T(8,128)(2,1)}) fusion(f32[4096]{0:T(1024)S(1)} %bitcast.20, f32[]{:T(128)} %bitcast.17, bf16[4096,512]{1,0:T(8,128)(2,1)} %all-gather.5.cloned.1.call-done, bf16[2048,512]{1,0:T(8,128)(2,1)} %param.6, f32[2048]{0:T(1024)S(1)} %add_rsqrt_fusion), kind=kOutput, calls=%fused_computation | convolution fusion | flops 8626632704 | bytes 23101444 | tf_op jit(solution)/shard_map/rd,ld->rl/dot_general | solution.py:16
  66.7 18.1 %all-gather.7.cloned.1.call-done = bf16[4096,128]{1,0:T(8,128)(2,1)} async-done(((bf16[256,128]{1,0:T(8,128)(2,1)}), bf16[4096,128]{1,0:T(8,128)(2,1)}) %all-gather.7.cloned.1.call-update) | async-done | bytes 1048592 | tf_op jit(solution)/shard_map/all_gather | solution.py:45
  84.8 11.6 %fusion.11 = f32[2048,128]{1,0:T(8,128)} fusion(bf16[4096,2048]{1,0:T(8,128)(2,1)} %get-tuple-element.12, bf16[4096,128]{1,0:T(8,128)(2,1)} %all-gather.7.cloned.1.call-done), kind=kOutput, calls=%fused_computation.35 | convolution fusion | flops 2147483648 | bytes 18874368 | tf_op jit(solution)/shard_map/rl,rv->lv/dot_general | solution.py:49
  96.4 0.0 all-reduce.5.cloned.1.call-update
  96.5 0.0 reduce-scatter.3.cloned.1.call-start
  96.5 69.1 %psum.59 = f32[128]{0:T(128)S(1)} all-reduce(f32[128]{0:T(128)S(1)} %get-tuple-element.13), channel_id=1, replica_groups=mesh['grp'=8,'lm'=16] {'grp','lm'}, use_global_device_ids=true, to_apply=%region_8.0 | all-reduce | flops 128 | bytes 1024 | tf_op jit(solution)/shard_map/psum | solution.py:44
  165.7 0.6 convert_reduce_fusion
  166.3 19.9 %all-reduce.1 = (f32[2048]{0:T(1024)S(1)}, f32[]{:T(128)}) all-reduce(f32[2048]{0:T(1024)S(1)} %get-tuple-element.11, f32[]{:T(128)} %convert_reduce_fusion), channel_id=1, replica_groups=mesh['grp'=8,'lm'=16] {'grp'}, use_global_device_ids=true, to_apply=%region_4.0 | all-reduce | flops 2049 | bytes 16392 | tf_op jit(solution)/shard_map/psum | solution.py:40
  186.2 0.6 broadcast_divide_fusion.1
  186.8 0.0 all-reduce.5.cloned.1.call-done
  186.9 1.8 convolution_bitcast_fusion.1
  188.7 0.0 copy-start
  188.7 12.0 %fusion.2 = f32[4096,128]{1,0:T(8,128)} fusion(bf16[4096,2048]{1,0:T(8,128)(2,1)} %get-tuple-element.12, f32[128]{0:T(128)S(1)} %convolution_bitcast_fusion.1, f32[4096]{0:T(1024)S(1)} %bitcast.21, f32[2048,128]{1,0:T(8,128)} %all-reduce.5.cloned.1.call-done, f32[128]{0:T(128)S(1)} %psum.59, f32[2048]{0:T(1024)S(1)} %broadcast_divide_fusion.1), kind=kOutput, calls=%fused_computation.8 | convolution fusion | flops 2149318656 | bytes 19948544 | tf_op jit(solution)/shard_map/dot_general | solution.py:60
  200.7 0.0 reduce-scatter.3.cloned.1.call-update
  200.7 0.0 all-gather.9.cloned.1.call-start
  200.7 61.7 %reduce-scatter.3.cloned.1.call-done = f32[256,128]{1,0:T(8,128)} async-done(((f32[4096,128]{1,0:T(8,128)}), f32[256,128]{1,0:T(8,128)}) %reduce-scatter.3.cloned.1.call-update) | async-done | bytes 131088 | tf_op jit(solution)/shard_map/reduce_scatter | solution.py:58
  262.4 0.0 copy-done
  262.4 1.0 multiply_reduce_fusion.2
  263.5 67.6 %all-reduce = (f32[128]{0:T(128)S(1)}, f32[128]{0:T(128)S(1)}) all-reduce(f32[128]{0:T(128)S(1)} %get-tuple-element.6, f32[128]{0:T(128)S(1)} %get-tuple-element.5), channel_id=1, replica_groups=mesh['grp'=8,'lm'=16] {'grp','lm'}, use_global_device_ids=true, to_apply=%region_11.0 | all-reduce | flops 256 | bytes 2048 | tf_op jit(solution)/shard_map/psum | solution.py:65
  331.1 1.6 multiply_convert_fusion
  332.8 0.0 all-gather.9.cloned.1.call-update
  332.8 0.3 all-reduce.7.cloned.1.call-start
  333.1 29.2 %all-gather.9.cloned.1.call-done = bf16[4096,128]{1,0:T(8,128)(2,1)} async-done(((bf16[256,128]{1,0:T(8,128)(2,1)}), bf16[4096,128]{1,0:T(8,128)(2,1)}) %all-gather.9.cloned.1.call-update) | async-done | bytes 1048592 | tf_op jit(solution)/shard_map/all_gather | solution.py:73
  362.2 11.6 %fusion.12 = f32[2048,128]{1,0:T(8,128)} fusion(bf16[4096,2048]{1,0:T(8,128)(2,1)} %get-tuple-element.12, bf16[4096,128]{1,0:T(8,128)(2,1)} %all-gather.9.cloned.1.call-done), kind=kOutput, calls=%fused_computation.36 | convolution fusion | flops 2147483648 | bytes 18874368 | tf_op jit(solution)/shard_map/rl,rv->lv/dot_general | solution.py:49
  373.9 0.0 all-reduce.7.cloned.1.call-update
  373.9 0.0 reduce-scatter.5.cloned.1.call-start
  373.9 83.7 %all-reduce.7.cloned.1.call-done = f32[2048,128]{1,0:T(8,128)} async-done(((f32[2048,128]{1,0:T(8,128)}), f32[2048,128]{1,0:T(8,128)}) %all-reduce.7.cloned.1.call-update) | async-done | bytes 1048592 | tf_op jit(solution)/shard_map/psum | solution.py:48
  457.6 1.8 convolution_bitcast_fusion
  459.4 12.0 %fusion.1 = f32[4096,128]{1,0:T(8,128)} fusion(bf16[4096,2048]{1,0:T(8,128)(2,1)} %get-tuple-element.12, f32[128]{0:T(128)S(1)} %convolution_bitcast_fusion, f32[4096]{0:T(1024)S(1)} %bitcast.22, f32[2048,128]{1,0:T(8,128)} %all-reduce.7.cloned.1.call-done, f32[128]{0:T(128)S(1)} %get-tuple-element.15, f32[2048]{0:T(1024)S(1)} %broadcast_divide_fusion.1), kind=kOutput, calls=%fused_computation.6 | convolution fusion | flops 2149318656 | bytes 19948544 | tf_op jit(solution)/shard_map/dot_general | solution.py:60
  471.4 0.0 reduce-scatter.5.cloned.1.call-update
  471.4 63.1 %reduce-scatter.5.cloned.1.call-done = f32[256,128]{1,0:T(8,128)} async-done(((f32[4096,128]{1,0:T(8,128)}), f32[256,128]{1,0:T(8,128)}) %reduce-scatter.5.cloned.1.call-update) | async-done | bytes 131088 | tf_op jit(solution)/shard_map/reduce_scatter | solution.py:58
  534.5 1.0 multiply_reduce_fusion.1
  535.4 68.2 %psum.63 = f32[128]{0:T(128)S(1)} all-reduce(f32[128]{0:T(128)S(1)} %multiply_reduce_fusion.1), channel_id=1, replica_groups=mesh['grp'=8,'lm'=16] {'grp','lm'}, use_global_device_ids=true, to_apply=%region_17.0 | all-reduce | flops 128 | bytes 1024 | tf_op jit(solution)/shard_map/psum | solution.py:65
  603.6 1.6 broadcast_divide_fusion
  (6 shorter events, 0.1 us)
Async XLA Ops:
  6.5 44.0 %all-gather.5.cloned.1.call-start = ((), (), s32[]{:S(2)}) async-start(), calls=%async_computation.2 | async-start | bytes 4456448 | tf_op jit(solution)/shard_map/all_gather | solution.py:32
  9.4 75.4 %all-gather.7.cloned.1.call-start = ((), (), s32[]{:S(2)}) async-start(), calls=%async_computation.3 | async-start | bytes 1114112 | tf_op jit(solution)/shard_map/all_gather | solution.py:45
  11.1 175.7 %all-reduce.5.cloned.1.call-start = ((), (), s32[]{:S(2)}) async-start(), calls=%async_computation.4 | async-start | bytes 2097152 | tf_op jit(solution)/shard_map/psum | solution.py:48
  96.5 166.0 %reduce-scatter.3.cloned.1.call-start = ((), (), s32[]{:S(2)}) async-start(), calls=%async_computation.5 | async-start | bytes 2228224 | tf_op jit(solution)/shard_map/reduce_scatter | solution.py:58
  188.7 73.8 %copy-start = (f32[256]{0:T(256)S(1)}, f32[256]{0:T(256)}, u32[]{:S(2)}) copy-start(f32[256]{0:T(256)} %param.8) | copy-start | bytes 3076
  200.7 161.5 %all-gather.9.cloned.1.call-start = ((), (), s32[]{:S(2)}) async-start(), calls=%async_computation.6 | async-start | bytes 1114112 | tf_op jit(solution)/shard_map/all_gather | solution.py:73
  332.8 124.8 %all-reduce.7.cloned.1.call-start = ((), (), s32[]{:S(2)}) async-start(), calls=%async_computation.7 | async-start | bytes 2097152 | tf_op jit(solution)/shard_map/psum | solution.py:48
  373.9 160.6 %reduce-scatter.5.cloned.1.call-start = ((), (), s32[]{:S(2)}) async-start(), calls=%async_computation.8 | async-start | bytes 2228224 | tf_op jit(solution)/shard_map/reduce_scatter | solution.py:58
Sparse Core Ops, SparseCore 0:
  9.5 40.9 all-gather.4
  52.3 32.5 all-gather.6
  96.6 84.5 all-reduce.4
  200.8 61.5 reduce-scatter.2
  332.9 29.2 all-gather.8
  374.0 83.5 all-reduce.6
  471.5 62.8 reduce-scatter.4
where the time goes:
time: 613 us; the launch traced here: 612 us
  waiting for transfers between devices  270 us (44%)
  blocking collectives  246 us (40%)
  matrix products  67 us (11%)
  between operations  14.2 us (2%)
  other arithmetic  13.8 us (2%)
    psum x2, blocking collectives, local(): lax.psum((jnp.sum(image * image, axis=0), jnp.sum(row_weight[:, None] * i...  136 us
    reduce_scatter x2, waiting for transfers between devices, local(): lax.psum_scatter(weights[:, None] * (jnp.dot(build_tile, side_b, preferre...  125 us
    psum x2, waiting for transfers between devices, local(): lax.psum(jnp.einsum('rl,rv->lv', build_tile, group_weighted, preferred_el...  83.7 us
    psum x1, blocking collectives, local(): totals = lax.psum(jnp.sum(weighted_full, axis=0), ('grp', 'lm'))  69.1 us
    all_gather x1, waiting for transfers between devices, local(): lax.all_gather((row_weight[:, None] * vectors).astype(jnp.bfloat16), 'lm'...  29.2 us
    dot_general x2, matrix products, local(): jnp.dot(build_tile, side_b, preferred_element_type=jnp.float32)  24 us
    dot_general x2, matrix products, local(): jnp.einsum('rl,rv->lv', build_tile, group_weighted, preferred_element_typ...  23.2 us
    all_gather x1, blocking collectives, local(): lax.all_gather(row_weight.astype(jnp.bfloat16), 'lm', axis=0, tiled=True)  21.3 us
  transfers between devices with their start and end apart: 7, of which 6 were waited for; matrix products, arithmetic and copies ran while one was open for 4% of the time, Pallas kernels for 0%

commit v1 on v0

--- a/solution.py
+++ b/solution.py
@@ -4,6 +4,10 @@
 from jax.sharding import PartitionSpec as P
 
 ITERS = 2
+
+
+def detail_the_bands(m):
+    return lax.psum(lax.psum(m, axis_name="grp"), axis_name="lm")
 
 
 def unit_rows(values):
@@ -62,9 +66,8 @@
             scatter_dimension=0,
             tiled=True,
         )
-        square, column = lax.psum(
-            (jnp.sum(image * image, axis=0), jnp.sum(row_weight[:, None] * image, axis=0)),
-            ("grp", "lm"),
+        square, column = detail_the_bands(
+            (jnp.sum(image * image, axis=0), jnp.sum(row_weight[:, None] * image, axis=0))
         )
         scale = jnp.sqrt(square / total_rows + 1e-06)
         vectors = image / scale[None, :]

time: 613 us -> 583 us (0.951)
  blocking collectives: 246 us -> 220 us
    psum x2 -> x4, blocking collectives: 136 us -> 110 us  [detail_the_bands(): return lax.psum(lax.psum(m, axis_name='grp'), axis_name='lm')]
where the time goes in v1:
time: 583 us; the launch traced here: 582 us
  waiting for transfers between devices  267 us (46%)
  blocking collectives  220 us (38%)
  matrix products  67 us (11%)
  between operations  14.2 us (2%)
  other arithmetic  13.8 us (2%)
    reduce_scatter x2, waiting for transfers between devices, local(): lax.psum_scatter(weights[:, None] * (jnp.dot(build_tile, side_b, preferre...  124 us
    psum x4, blocking collectives, detail_the_bands(): return lax.psum(lax.psum(m, axis_name='grp'), axis_name='lm')  110 us
    psum x2, waiting for transfers between devices, local(): lax.psum(jnp.einsum('rl,rv->lv', build_tile, group_weighted, preferred_el...  83.4 us
    psum x1, blocking collectives, local(): totals = lax.psum(jnp.sum(weighted_full, axis=0), ('grp', 'lm'))  69.1 us
    all_gather x1, waiting for transfers between devices, local(): lax.all_gather((row_weight[:, None] * vectors).astype(jnp.bfloat16), 'lm'...  26.3 us
    dot_general x2, matrix products, local(): jnp.dot(build_tile, side_b, preferred_element_type=jnp.float32)  24 us
    dot_general x2, matrix products, local(): jnp.einsum('rl,rv->lv', build_tile, group_weighted, preferred_element_typ...  23.2 us
    all_gather x1, blocking collectives, local(): lax.all_gather(row_weight.astype(jnp.bfloat16), 'lm', axis=0, tiled=True)  21.3 us
  transfers between devices with their start and end apart: 7, of which 6 were waited for; matrix products, arithmetic and copies ran while one was open for 4% of the time, Pallas kernels for 0%

profile of v1, /device:TPU:1, one launch (start us, length us, event | category | flops | bytes accessed | tf_op | source)
XLA Modules:
  0.0 582.2 jit_solution(3792912268493922208)
XLA Ops:
  6.5 0.0 all-gather.5.cloned.1.call-start
  6.5 1.1 fusion.8
  7.6 1.8 fusion.9
  9.4 0.0 all-gather.5.cloned.1.call-update
  9.4 0.0 all-gather.7.cloned.1.call-start
  9.5 1.6 multiply_reduce_fusion.4
  11.1 0.0 all-gather.7.cloned.1.call-update
  11.1 0.0 all-reduce.6.cloned.1.call-start
  11.2 2.1 fusion.3
  13.3 0.7 convert_element_type.35
  14.0 21.3 %all-gather = bf16[16,1,256]{2,1,0:T(2,128)(2,1)S(1)} all-gather(bf16[1,1,256]{2,1,0:T(2,128)(2,1)S(1)} %reshape.21), channel_id=1, replica_groups=mesh['grp'=8,'lm'=16] {'lm'}, dimensions={0}, use_global_device_ids=true | all-gather | bytes 8704 | tf_op jit(solution)/shard_map/all_gather | solution.py:37
  36.0 14.6 %all-gather.5.cloned.1.call-done = bf16[4096,512]{1,0:T(8,128)(2,1)} async-done(((bf16[256,512]{1,0:T(8,128)(2,1)}), bf16[4096,512]{1,0:T(8,128)(2,1)}) %all-gather.5.cloned.1.call-update) | async-done | bytes 4194320 | tf_op jit(solution)/shard_map/all_gather | solution.py:36
  50.6 16.2 %multiply_reduce_fusion = (f32[2048]{0:T(1024)S(1)}, bf16[4096,2048]{1,0:T(8,128)(2,1)}) fusion(f32[4096]{0:T(1024)S(1)} %bitcast.20, f32[]{:T(128)} %bitcast.17, bf16[4096,512]{1,0:T(8,128)(2,1)} %all-gather.5.cloned.1.call-done, bf16[2048,512]{1,0:T(8,128)(2,1)} %param.6, f32[2048]{0:T(1024)S(1)} %add_rsqrt_fusion), kind=kOutput, calls=%fused_computation | convolution fusion | flops 8626632704 | bytes 23101444 | tf_op jit(solution)/shard_map/rd,ld->rl/dot_general | solution.py:20
  66.7 18.1 %all-gather.7.cloned.1.call-done = bf16[4096,128]{1,0:T(8,128)(2,1)} async-done(((bf16[256,128]{1,0:T(8,128)(2,1)}), bf16[4096,128]{1,0:T(8,128)(2,1)}) %all-gather.7.cloned.1.call-update) | async-done | bytes 1048592 | tf_op jit(solution)/shard_map/all_gather | solution.py:49
  84.8 11.6 %fusion.11 = f32[2048,128]{1,0:T(8,128)} fusion(bf16[4096,2048]{1,0:T(8,128)(2,1)} %get-tuple-element.14, bf16[4096,128]{1,0:T(8,128)(2,1)} %all-gather.7.cloned.1.call-done), kind=kOutput, calls=%fused_computation.35 | convolution fusion | flops 2147483648 | bytes 18874368 | tf_op jit(solution)/shard_map/rl,rv->lv/dot_general | solution.py:53
  96.4 0.0 all-reduce.6.cloned.1.call-update
  96.5 0.0 reduce-scatter.3.cloned.1.call-start
  96.5 69.1 %psum.80 = f32[128]{0:T(128)S(1)} all-reduce(f32[128]{0:T(128)S(1)} %get-tuple-element.15), channel_id=1, replica_groups=mesh['grp'=8,'lm'=16] {'grp','lm'}, use_global_device_ids=true, to_apply=%region_8.0 | all-reduce | flops 128 | bytes 1024 | tf_op jit(solution)/shard_map/psum | solution.py:48
  165.7 0.6 convert_reduce_fusion
  166.3 19.9 %all-reduce.2 = (f32[2048]{0:T(1024)S(1)}, f32[]{:T(128)}) all-reduce(f32[2048]{0:T(1024)S(1)} %get-tuple-element.13, f32[]{:T(128)} %convert_reduce_fusion), channel_id=1, replica_groups=mesh['grp'=8,'lm'=16] {'grp'}, use_global_device_ids=true, to_apply=%region_4.0 | all-reduce | flops 2049 | bytes 16392 | tf_op jit(solution)/shard_map/psum | solution.py:44
  186.2 0.6 broadcast_divide_fusion.1
  186.8 0.0 all-reduce.6.cloned.1.call-done
  186.9 1.8 convolution_bitcast_fusion.1
  188.7 0.0 copy-start
  188.7 12.0 %fusion.2 = f32[4096,128]{1,0:T(8,128)} fusion(bf16[4096,2048]{1,0:T(8,128)(2,1)} %get-tuple-element.14, f32[128]{0:T(128)S(1)} %convolution_bitcast_fusion.1, f32[4096]{0:T(1024)S(1)} %bitcast.21, f32[2048,128]{1,0:T(8,128)} %all-reduce.6.cloned.1.call-done, f32[128]{0:T(128)S(1)} %psum.80, f32[2048]{0:T(1024)S(1)} %broadcast_divide_fusion.1), kind=kOutput, calls=%fused_computation.8 | convolution fusion | flops 2149318656 | bytes 19948544 | tf_op jit(solution)/shard_map/dot_general | solution.py:64
  200.7 0.0 reduce-scatter.3.cloned.1.call-update
  200.7 0.0 all-gather.9.cloned.1.call-start
  200.7 61.1 %reduce-scatter.3.cloned.1.call-done = f32[256,128]{1,0:T(8,128)} async-done(((f32[4096,128]{1,0:T(8,128)}), f32[256,128]{1,0:T(8,128)}) %reduce-scatter.3.cloned.1.call-update) | async-done | bytes 131088 | tf_op jit(solution)/shard_map/reduce_scatter | solution.py:62
  261.9 0.0 copy-done
  261.9 1.0 multiply_reduce_fusion.2
  262.9 20.7 %all-reduce.1 = (f32[128]{0:T(128)S(1)}, f32[128]{0:T(128)S(1)}) all-reduce(f32[128]{0:T(128)S(1)} %get-tuple-element.6, f32[128]{0:T(128)S(1)} %get-tuple-element.5), channel_id=1, replica_groups=mesh['grp'=8,'lm'=16] {'grp'}, use_global_device_ids=true, to_apply=%region_11.0 | all-reduce | flops 256 | bytes 2048 | tf_op jit(solution)/shard_map/psum | solution.py:10
  283.6 34.4 %all-reduce = (f32[128]{0:T(128)S(1)}, f32[128]{0:T(128)S(1)}) all-reduce(f32[128]{0:T(128)S(1)} %get-tuple-element.9, f32[128]{0:T(128)S(1)} %get-tuple-element.10), channel_id=1, replica_groups=mesh['grp'=8,'lm'=16] {'lm'}, use_global_device_ids=true, to_apply=%region_12.0 | all-reduce | flops 256 | bytes 2048 | tf_op jit(solution)/shard_map/psum | solution.py:10
  318.0 1.6 multiply_convert_fusion
  319.6 0.0 all-gather.9.cloned.1.call-update
  319.7 0.0 all-reduce.8.cloned.1.call-start
  319.7 26.3 %all-gather.9.cloned.1.call-done = bf16[4096,128]{1,0:T(8,128)(2,1)} async-done(((bf16[256,128]{1,0:T(8,128)(2,1)}), bf16[4096,128]{1,0:T(8,128)(2,1)}) %all-gather.9.cloned.1.call-update) | async-done | bytes 1048592 | tf_op jit(solution)/shard_map/all_gather | solution.py:76
  346.0 11.6 %fusion.12 = f32[2048,128]{1,0:T(8,128)} fusion(bf16[4096,2048]{1,0:T(8,128)(2,1)} %get-tuple-element.14, bf16[4096,128]{1,0:T(8,128)(2,1)} %all-gather.9.cloned.1.call-done), kind=kOutput, calls=%fused_computation.36 | convolution fusion | flops 2147483648 | bytes 18874368 | tf_op jit(solution)/shard_map/rl,rv->lv/dot_general | solution.py:53
  357.6 0.0 all-reduce.8.cloned.1.call-update
  357.7 0.3 reduce-scatter.5.cloned.1.call-start
  357.9 83.4 %all-reduce.8.cloned.1.call-done = f32[2048,128]{1,0:T(8,128)} async-done(((f32[2048,128]{1,0:T(8,128)}), f32[2048,128]{1,0:T(8,128)}) %all-reduce.8.cloned.1.call-update) | async-done | bytes 1048592 | tf_op jit(solution)/shard_map/psum | solution.py:52
  441.3 1.8 convolution_bitcast_fusion
  443.1 12.0 %fusion.1 = f32[4096,128]{1,0:T(8,128)} fusion(bf16[4096,2048]{1,0:T(8,128)(2,1)} %get-tuple-element.14, f32[128]{0:T(128)S(1)} %convolution_bitcast_fusion, f32[4096]{0:T(1024)S(1)} %bitcast.22, f32[2048,128]{1,0:T(8,128)} %all-reduce.8.cloned.1.call-done, f32[128]{0:T(128)S(1)} %get-tuple-element.17, f32[2048]{0:T(1024)S(1)} %broadcast_divide_fusion.1), kind=kOutput, calls=%fused_computation.6 | convolution fusion | flops 2149318656 | bytes 19948544 | tf_op jit(solution)/shard_map/dot_general | solution.py:64
  455.1 0.0 reduce-scatter.5.cloned.1.call-update
  455.2 63.0 %reduce-scatter.5.cloned.1.call-done = f32[256,128]{1,0:T(8,128)} async-done(((f32[4096,128]{1,0:T(8,128)}), f32[256,128]{1,0:T(8,128)}) %reduce-scatter.5.cloned.1.call-update) | async-done | bytes 131088 | tf_op jit(solution)/shard_map/reduce_scatter | solution.py:62
  518.2 1.0 multiply_reduce_fusion.1
  519.2 20.6 %psum.86 = f32[128]{0:T(128)S(1)} all-reduce(f32[128]{0:T(128)S(1)} %multiply_reduce_fusion.1), channel_id=1, replica_groups=mesh['grp'=8,'lm'=16] {'grp'}, use_global_device_ids=true, to_apply=%region_19.0 | all-reduce | flops 128 | bytes 1024 | tf_op jit(solution)/shard_map/psum | solution.py:10
  539.7 34.0 %psum.87 = f32[128]{0:T(128)S(1)} all-reduce(f32[128]{0:T(128)S(1)} %psum.86), channel_id=1, replica_groups=mesh['grp'=8,'lm'=16] {'lm'}, use_global_device_ids=true, to_apply=%region_20.0 | all-reduce | flops 128 | bytes 1024 | tf_op jit(solution)/shard_map/psum | solution.py:10
  573.8 1.6 broadcast_divide_fusion
  (6 shorter events, 0.1 us)
Async XLA Ops:
  6.5 44.0 %all-gather.5.cloned.1.call-start = ((), (), s32[]{:S(2)}) async-start(), calls=%async_computation.2 | async-start | bytes 4456448 | tf_op jit(solution)/shard_map/all_gather | solution.py:36
  9.4 75.4 %all-gather.7.cloned.1.call-start = ((), (), s32[]{:S(2)}) async-start(), calls=%async_computation.3 | async-start | bytes 1114112 | tf_op jit(solution)/shard_map/all_gather | solution.py:49
  11.1 175.7 %all-reduce.6.cloned.1.call-start = ((), (), s32[]{:S(2)}) async-start(), calls=%async_computation.4 | async-start | bytes 2097152 | tf_op jit(solution)/shard_map/psum | solution.py:52
  96.5 165.4 %reduce-scatter.3.cloned.1.call-start = ((), (), s32[]{:S(2)}) async-start(), calls=%async_computation.5 | async-start | bytes 2228224 | tf_op jit(solution)/shard_map/reduce_scatter | solution.py:62
  188.7 73.2 %copy-start = (f32[256]{0:T(256)S(1)}, f32[256]{0:T(256)}, u32[]{:S(2)}) copy-start(f32[256]{0:T(256)} %param.8) | copy-start | bytes 3076
  200.7 145.3 %all-gather.9.cloned.1.call-start = ((), (), s32[]{:S(2)}) async-start(), calls=%async_computation.6 | async-start | bytes 1114112 | tf_op jit(solution)/shard_map/all_gather | solution.py:76
  319.7 121.7 %all-reduce.8.cloned.1.call-start = ((), (), s32[]{:S(2)}) async-start(), calls=%async_computation.7 | async-start | bytes 2097152 | tf_op jit(solution)/shard_map/psum | solution.py:52
  357.7 160.6 %reduce-scatter.5.cloned.1.call-start = ((), (), s32[]{:S(2)}) async-start(), calls=%async_computation.8 | async-start | bytes 2228224 | tf_op jit(solution)/shard_map/reduce_scatter | solution.py:62
Sparse Core Ops, SparseCore 0:
  9.5 40.9 all-gather.4
  52.3 32.5 all-gather.6
  96.6 84.5 all-reduce.5
  200.8 60.9 reduce-scatter.2
  319.8 26.1 all-gather.8
  357.8 83.5 all-reduce.7
  455.3 62.8 reduce-scatter.4
